TPU v7x, 32 devices: a whole 2x2x4 slice. The times are simulated.
32 devices in a mesh: groups: 2 (over x), tensor: 16 (over z, y, core).
Axes of the slice: x: 2, y: 2, z: 4, core: 2. Of those that a mesh axis runs over, the one named last changes fastest.
Arguments:
- hidden: bfloat16 [384, 16384], P('groups', 'tensor'), parts along dimension 0, may hold values from -6 to 6
- w_query: bfloat16 [16384, 8192], P(None, 'tensor'), may hold values from -0.046875 to 0.046875
- w_out: bfloat16 [8192, 16384], P('tensor'), may hold values from -0.09375 to 0.09375
- new_kv: bfloat16 [384, 2, 4, 128], P(('groups', 'tensor')), parts along dimension 0, may hold values from -6 to 6
- prefix_kv: bfloat16 [32, 3, 2, 4, 512, 128], P(('groups', 'tensor')), parts along dimension 0, may hold values from -700 to 700
- suffix_kv: bfloat16 [384, 2, 4, 256, 128], P(('groups', 'tensor')), parts along dimension 0, may hold values from -6 to 6
- parents: int32 [384], P(('groups', 'tensor')), parts along dimension 0, may hold values from 0 to 7
- lengths: int32 [384], P(('groups', 'tensor')), parts along dimension 0, may hold values from 1 to 256, 36864 in all
Outputs:
- attended: bfloat16 [384, 16384], P('groups', 'tensor'), parts along dimension 0
There are 2 independent parts, one for each index of `groups`. A program takes and returns all parts, laid end to end along the dimension named above; an argument that names none is the same for every part. Nothing has to cross between parts.
Inputs may be any that keep to these rules, and one draw needn't show every extreme that they name: `lengths`: some page is full.
All inputs are finite; a program needn't handle non-finite values. No bound on the sum of `lengths` on one device may be relied on, other than what follows from the above.
Results may differ from a plain program's by a relative error of at most 0.02.
The roundings to bfloat16 on the way count: a program that leaves them out, or rounds other values in their place, can miss the bound.
Values may be sent and summed in bfloat16 or wider, within the bound.
No kernel may reach another device: no remote copies, remote signals or barrier semaphores. Data moves between devices by JAX's collectives and lax.ppermute only.
A program may use at most 192 MiB of HBM per device.

v0:
```python
import jax
import jax.numpy as jnp
from jax import lax
from jax.sharding import PartitionSpec as P

HEADS = 64
KV = 4
HD = 128
BEAMS = 8
big_negative = -1e30
rope_base = 500000.0


def swapped(block, axis, apart):
    count = lax.axis_size(axis)
    route = []
    for low in range(count):
        high = low | 1 << apart
        if high != low and high < count:
            route += [(low, high), (high, low)]
    return lax.ppermute(block, axis, route)


def rotate(queries, position):
    half_size = HD // 2
    frequency = rope_base ** (-jnp.arange(half_size, dtype=jnp.float32) * 2.0 / HD)
    angles = position.astype(jnp.float32)[..., None, None] * frequency
    cosine = jnp.cos(angles)
    sines = jnp.sin(angles)
    entries = queries.astype(jnp.float32)
    lower_half = entries[..., :half_size]
    upper_half = entries[..., half_size:]
    turned = jnp.concatenate(
        [lower_half * cosine - upper_half * sines, upper_half * cosine + lower_half * sines],
        axis=-1,
    )
    return (turned * HD ** (-0.5)).astype(jnp.bfloat16)


def shared_part(grouped, key_block, value_block):
    scores = jnp.einsum("pbkge,pkne->pbkgn", grouped, key_block, preferred_element_type=jnp.float32)
    highest = jnp.max(scores, axis=-1)
    weights = jnp.exp(scores - highest[..., None])
    weight_sum = jnp.sum(weights, axis=-1)
    weighted = jnp.einsum(
        "pbkgn,pkne->pbkge",
        weights.astype(jnp.bfloat16),
        value_block,
        preferred_element_type=jnp.float32,
    )
    return (highest, weight_sum, weighted)


def own_part(grouped, key_block, value_block, usable):
    scores = jnp.einsum(
        "pbkge,pbkse->pbkgs", grouped, key_block, preferred_element_type=jnp.float32
    )
    usable_mask = usable[:, :, None, None, :]
    highest = jnp.max(jnp.where(usable_mask, scores, big_negative), axis=-1)
    weights = jnp.where(usable_mask, jnp.exp(scores - highest[..., None]), 0.0)
    weight_sum = jnp.sum(weights, axis=-1)
    weighted = jnp.einsum(
        "pbkgs,pbkse->pbkge",
        weights.astype(jnp.bfloat16),
        value_block,
        preferred_element_type=jnp.float32,
    )
    return (highest, weight_sum, weighted)


def combine(left_state, right_state):
    highest = jnp.maximum(left_state[0], right_state[0])
    left_factor = jnp.exp(left_state[0] - highest)
    right_factor = jnp.exp(right_state[0] - highest)
    weight_sum = left_state[1] * left_factor + right_state[1] * right_factor
    weighted = left_state[2] * left_factor[..., None] + right_state[2] * right_factor[..., None]
    return (highest, weight_sum, weighted)


def body(hidden, w_query, w_out, new_kv, prefix_kv, suffix_kv, parents, lengths):
    pair_side = lax.axis_index("tensor") % 2
    rows_here = new_kv.shape[0]
    half_beams = BEAMS // 2
    prompts_here = rows_here // half_beams
    prefix_len = 2 * prefix_kv.shape[4]
    page_size = suffix_kv.shape[3]
    per_kv = HEADS // KV

    def in_order(own_part_rows, far_rows, along):
        lower_part = jnp.where(pair_side == 0, own_part_rows, far_rows)
        upper_part = jnp.where(pair_side == 0, far_rows, own_part_rows)
        return jnp.concatenate([lower_part, upper_part], axis=along)

    query = jnp.dot(
        lax.all_gather(hidden, "tensor", axis=1, tiled=True),
        w_query,
        preferred_element_type=jnp.float32,
    ).astype(jnp.bfloat16)
    local_q = lax.all_to_all(query, "tensor", split_axis=0, concat_axis=1, tiled=True)
    local_q = local_q.reshape(prompts_here, half_beams, HEADS, HD)
    own_par = parents.reshape(prompts_here, half_beams)
    own_len = lengths.reshape(prompts_here, half_beams)
    own_pages = suffix_kv.reshape(prompts_here, half_beams, 2, KV, page_size, HD)
    new_pair = new_kv.reshape(prompts_here, half_beams, 2, KV, HD)
    positions = jnp.arange(page_size)
    far_prefix, far_pages, far_len = swapped((prefix_kv, suffix_kv, lengths), "tensor", 0)
    prefix_full = in_order(prefix_kv[0], far_prefix[0], 3)
    pages_all = in_order(own_pages, far_pages.reshape(own_pages.shape), 1)
    len_all = in_order(own_len, far_len.reshape(own_len.shape), 1)
    chosen = jnp.take_along_axis(pages_all, own_par[:, :, None, None, None, None], axis=1)
    page_len = jnp.take_along_axis(len_all, own_par, axis=1)
    grouped = rotate(local_q, prefix_len + page_len).reshape(
        prompts_here, half_beams, KV, per_kv, HD
    )
    prefix_state = shared_part(grouped, prefix_full[:, 0], prefix_full[:, 1])
    usable = positions[None, None, :] < page_len[:, :, None]
    suffix_state = own_part(grouped, chosen[:, :, 0], chosen[:, :, 1], usable)
    merged = combine(prefix_state, suffix_state)
    new_scores = jnp.einsum(
        "pbkge,pbke->pbkg", grouped, new_pair[:, :, 0], preferred_element_type=jnp.float32
    )
    new_values = jnp.broadcast_to(
        new_pair[:, :, 1].astype(jnp.float32)[:, :, :, None, :], grouped.shape
    )
    new_state = (new_scores, jnp.ones_like(new_scores), new_values)
    highest, weight_sum, weighted = combine(merged, new_state)
    heads_out = (
        (weighted / weight_sum[..., None]).astype(jnp.bfloat16).reshape(rows_here, HEADS * HD)
    )
    heads_view = lax.all_to_all(heads_out, "tensor", split_axis=1, concat_axis=0, tiled=True)
    projected = jnp.dot(heads_view, w_out, preferred_element_type=jnp.float32)
    summed = lax.psum_scatter(
        projected.astype(jnp.bfloat16), "tensor", scatter_dimension=1, tiled=True
    )
    return summed


def solution(mesh):
    return jax.shard_map(
        body,
        mesh=mesh,
        in_specs=(
            P("groups", "tensor"),
            P(None, "tensor"),
            P("tensor", None),
            P(("groups", "tensor"), None, None, None),
            P(("groups", "tensor"), None, None, None, None, None),
            P(("groups", "tensor"), None, None, None, None),
            P(("groups", "tensor")),
            P(("groups", "tensor")),
        ),
        out_specs=P("groups", "tensor"),
        check_vma=False,
    )
```

profile of v0, /device:TPU:0, one launch (start us, length us, event | category | flops | bytes accessed | tf_op | source)
XLA Modules:
  0.0 227.0 jit_solution(14612947954421246856)
XLA Ops:
  6.5 0.0 all-gather.2.cloned.1.call-start
  6.6 0.7 all-gather.2.cloned.1.call-update
  7.3 0.5 collective-permute-start.2
  7.8 3.9 %copy.48 = bf16[1,3,2,4,512,128]{5,4,3,1,2,0:T(8,128)(2,1)} copy(bf16[1,3,2,4,512,128]{5,4,3,2,1,0:T(8,128)(2,1)} %param.12) | data formatting | bytes 6291456 | tf_op args[4]
  11.6 0.2 collective-permute-start
  11.8 0.0 copy-done.6
  11.8 0.3 collective-permute-start.1
  12.2 0.0 copy-done.5
  12.2 0.1 reshape.192
  12.2 0.1 reshape.191
  12.3 0.1 reshape.196
  12.4 0.0 copy-done.3
  12.4 0.6 fusion.75
  13.1 0.6 fusion.67
  13.7 3.9 %collective-permute-done.1 = s32[12]{0:T(128)S(1)} collective-permute-done((s32[12]{0:T(128)S(1)}, s32[12]{0:T(128)S(1)}, u32[]{:S(2)}, u32[]{:S(2)}) %collective-permute-start.1) | collective-permute-done | bytes 80 | tf_op jit(solution)/shard_map/ppermute | solution.py:21
  17.6 0.1 select_n.128
  17.7 0.1 select_n.126
  17.7 0.1 pad_add_fusion
  17.8 0.7 gather_fusion
  18.6 0.1 reshape.199
  18.7 0.1 iota_compare_fusion
  18.7 0.7 multiply_cosine_fusion
  19.5 3.0 %collective-permute-done = bf16[1,3,2,4,512,128]{5,4,3,1,2,0:T(8,128)(2,1)} collective-permute-done((bf16[1,3,2,4,512,128]{5,4,3,1,2,0:T(8,128)(2,1)}, bf16[1,3,2,4,512,128]{5,4,3,1,2,0:T(8,128)(2,1)}, u32[]{:S(2)}, u32[]{:S(2)}) %collective-permute-start) | collective-permute-done | bytes 3145760 | tf_op jit(solution)/shard_map/ppermute | solution.py:21
  22.4 0.0 copy-done
  22.4 5.0 %select_bitcast_fusion.1 = (bf16[3,2,4,512,128]{4,3,2,0,1:T(8,128)(2,1)}, bf16[3,2,4,512,128]{4,3,2,0,1:T(8,128)(2,1)}) fusion(bf16[1,3,2,4,512,128]{5,4,3,1,2,0:T(8,128)(2,1)} %collective-permute-done, pred[]{:T(512)S(6)} %eq.4, bf16[1,3,2,4,512,128]{5,4,3,2,1,0:T(8,128)(2,1)S(1)} %copy-done), kind=kLoop, calls=%fused_computation.24 | loop fusion | flops 3145728 | bytes 12582913 | tf_op jit(solution)/shard_map/jit(_where)/select_n | solution.py:90
  27.5 0.0 collective-permute-done.2
  27.5 0.0 slice-done.2
  27.5 0.0 slice-done.3
  27.5 3.9 %broadcast_select_fusion.1 = (bf16[12,2,4,256,128]{4,3,2,1,0:T(8,128)(2,1)S(1)}, bf16[12,2,4,256,128]{4,3,2,1,0:T(8,128)(2,1)S(1)}) fusion(bf16[12,2,4,256,128]{4,3,2,1,0:T(8,128)(2,1)S(1)} %bitcast.116, bf16[12,2,4,256,128]{4,3,2,1,0:T(8,128)(2,1)} %collective-permute-done.2, pred[]{:T(512)S(6)} %eq.4), kind=kLoop, calls=%fused_computation.7 | loop fusion | flops 6291456 | bytes 25165824 | tf_op jit(solution)/shard_map/jit(_where)/select_n | solution.py:90
  31.4 5.3 %pad_maximum_fusion = bf16[3,8,2,4,256,128]{5,4,3,2,1,0:T(8,128)(2,1)} fusion(bf16[3,4,2,4,256,128]{5,4,3,2,1,0:T(8,128)(2,1)S(1)} %bitcast.112, bf16[3,4,2,4,256,128]{5,4,3,2,1,0:T(8,128)(2,1)S(1)} %bitcast.111), kind=kLoop, calls=%fused_computation.3 | loop fusion | flops 6291456 | bytes 25165824 | tf_op jit(solution)/shard_map/concatenate | solution.py:92
  36.6 8.8 %gather_fusion.1 = bf16[12,2,4,256,128]{4,3,2,1,0:T(8,128)(2,1)} fusion(bf16[3,8,2,4,256,128]{5,4,3,2,1,0:T(8,128)(2,1)} %pad_maximum_fusion, s32[12]{0:T(128)S(1)} %reshape.196), kind=kCustom, calls=%fused_computation.1 | custom fusion | bytes 12583008 | tf_op jit(solution)/shard_map/jit(take_along_axis)/gather | solution.py:110
  45.4 6.2 %copy.53 = bf16[12,2,4,256,128]{4,3,2,0,1:T(8,128)(2,1)} copy(bf16[12,2,4,256,128]{4,3,2,1,0:T(8,128)(2,1)} %gather_fusion.1) | data formatting | bytes 12582912 | tf_op jit(solution)/shard_map/jit(take_along_axis)/gather | solution.py:110
  51.7 22.6 %all-gather.2.cloned.1.call-done = bf16[192,16384]{1,0:T(8,128)(2,1)} async-done(((bf16[192,1024]{1,0:T(8,128)(2,1)}), bf16[192,16384]{1,0:T(8,128)(2,1)}) %all-gather.2.cloned.1.call-update) | async-done | bytes 6291472 | tf_op jit(solution)/shard_map/all_gather | solution.py:95
  74.2 11.0 %convolution_convert_fusion.1 = bf16[192,512]{1,0:T(8,128)(2,1)S(1)} fusion(bf16[192,16384]{1,0:T(8,128)(2,1)} %all-gather.2.cloned.1.call-done, bf16[16384,512]{1,0:T(8,128)(2,1)} %param.9), kind=kOutput, calls=%fused_computation.35 | convolution fusion | flops 3221323776 | bytes 23265280 | tf_op jit(solution)/shard_map/dot_general | solution.py:94
  85.2 0.7 all_to_all.24
  86.0 3.5 %all-to-all-start = ((bf16[16,12,512]{2,1,0:T(8,128)(2,1)}), bf16[16,12,512]{2,1,0:T(8,128)(2,1)S(1)}, u32[]{:S(2)}, u32[]{:S(2)}) async-start(bf16[16,12,512]{2,1,0:T(8,128)(2,1)} %all_to_all.24), calls=%async_computation | async-start | bytes 524288 | tf_op jit(solution)/shard_map/all_to_all | solution.py:99
  89.5 0.0 reduce-scatter.2.cloned.1.call-start
  89.6 6.1 %broadcast_select_fusion.2 = bf16[3,4,2,4,256,128]{5,4,3,1,0,2:T(8,128)(2,1)} fusion(bf16[3,4,2,4,256,128]{5,4,3,1,0,2:T(8,128)(2,1)} %bitcast.110, pred[3,4]{1,0:T(4,128)(4,1)S(1)} %get-tuple-element.12), kind=kLoop, calls=%fused_computation.8 | loop fusion | flops 3145728 | bytes 12582924 | tf_op jit(solution)/shard_map/jit(take_along_axis)/select_n | solution.py:110
  95.7 3.8 %all-to-all-done = bf16[16,12,512]{2,1,0:T(8,128)(2,1)S(1)} async-done(((bf16[16,12,512]{2,1,0:T(8,128)(2,1)}), bf16[16,12,512]{2,1,0:T(8,128)(2,1)S(1)}, u32[]{:S(2)}, u32[]{:S(2)}) %all-to-all-start) | async-done | bytes 196640 | tf_op jit(solution)/shard_map/all_to_all | solution.py:99
  99.6 1.0 copy.50
  100.6 1.0 reshape.194
  101.6 0.0 copy-start.2
  101.6 1.0 multiply_subtract_fusion
  102.6 0.2 fusion.56
  102.8 0.9 fusion.58
  103.7 2.9 %select_reduce_fusion = (f32[3,4,4,16]{3,2,1,0:T(4,128)S(1)}, f32[3,4,4,16,256]{4,3,2,1,0:T(8,128)S(1)}) fusion(pred[3,4,256]{2,1,0:T(4,128)(4,1)S(1)} %iota_compare_fusion, bf16[3,4,2,4,256,128]{5,4,3,1,0,2:T(8,128)(2,1)} %broadcast_select_fusion.2, bf16[3,4,4,16,128]{4,3,1,2,0:T(8,128)(2,1)S(1)} %fusion.56), kind=kOutput, calls=%fused_computation.39 | convolution fusion | flops 50724096 | bytes 4134912 | tf_op jit(solution)/shard_map/pbkge,pbkse->pbkgs/dot_general | solution.py:55
  106.6 0.0 slice-start
  106.7 0.4 fusion.54
  107.0 0.0 copy-done.1
  107.0 0.0 copy-done.2
  107.0 0.0 slice-start.1
  107.0 1.3 bitcast_reduce_fusion
  108.4 0.7 fusion.12
  109.1 0.0 slice-done
  109.1 0.5 slice-done.1
  109.6 0.5 fusion.21
  110.1 0.0 copy-done.4
  110.2 1.3 fusion.49
  111.4 0.1 all_to_all.26
  111.6 0.1 copy.61
  111.7 12.8 %all_to_all.32 = bf16[12,16,512]{2,0,1:T(8,128)(2,1)S(1)} all-to-all(bf16[12,16,512]{2,0,1:T(8,128)(2,1)S(1)} %copy.61), channel_id=1, replica_groups=mesh['groups'=2,'tensor'=16] {'tensor'}, dimensions={1} | all-to-all | bytes 393216 | tf_op jit(solution)/shard_map/all_to_all | solution.py:130
  124.6 11.9 %convolution_convert_fusion = bf16[192,16384]{1,0:T(8,128)(2,1)} fusion(bf16[192,512]{1,0:T(8,128)(2,1)S(1)} %all_to_all.29, bf16[512,16384]{1,0:T(8,128)(2,1)} %param.10), kind=kOutput, calls=%fused_computation.2 | convolution fusion | flops 3224371200 | bytes 23265280 | tf_op jit(solution)/shard_map/dot_general | solution.py:131
  136.4 0.0 reduce-scatter.2.cloned.1.call-update
  136.5 83.7 %reduce-scatter.2.cloned.1.call-done = bf16[192,1024]{1,0:T(8,128)(2,1)} async-done(((bf16[192,16384]{1,0:T(8,128)(2,1)}), bf16[192,1024]{1,0:T(8,128)(2,1)}) %reduce-scatter.2.cloned.1.call-update) | async-done | bytes 393232 | tf_op jit(solution)/shard_map/reduce_scatter | solution.py:132
  (18 shorter events, 0.2 us)
Async XLA Ops:
  6.5 15.9 %copy-start = (bf16[1,3,2,4,512,128]{5,4,3,2,1,0:T(8,128)(2,1)S(1)}, bf16[1,3,2,4,512,128]{5,4,3,2,1,0:T(8,128)(2,1)}, u32[]{:S(2)}) copy-start(bf16[1,3,2,4,512,128]{5,4,3,2,1,0:T(8,128)(2,1)} %param.12) | copy-start | bytes 9437188
  6.5 5.3 %copy-start.6 = (s32[12]{0:T(128)S(1)}, s32[12]{0:T(128)}, u32[]{:S(2)}) copy-start(s32[12]{0:T(128)} %param.15) | copy-start | bytes 148
  6.5 5.6 %copy-start.5 = (s32[12]{0:T(128)S(1)}, s32[12]{0:T(128)}, u32[]{:S(2)}) copy-start(s32[12]{0:T(128)} %param.14) | copy-start | bytes 148
  6.5 5.9 %copy-start.3 = (bf16[12,2,4,128]{3,2,1,0:T(4,128)(2,1)S(1)}, bf16[12,2,4,128]{3,2,1,0:T(4,128)(2,1)}, u32[]{:S(2)}) copy-start(bf16[12,2,4,128]{3,2,1,0:T(4,128)(2,1)} %param.11) | copy-start | bytes 73732
  6.5 67.7 %all-gather.2.cloned.1.call-start = ((), (), s32[]{:S(2)}) async-start(), calls=%async_computation.3 | async-start | bytes 6684672 | tf_op jit(solution)/shard_map/all_gather | solution.py:95
  7.3 20.2 %collective-permute-start.2 = (bf16[12,2,4,256,128]{4,3,2,1,0:T(8,128)(2,1)}, bf16[12,2,4,256,128]{4,3,2,1,0:T(8,128)(2,1)}, u32[]{:S(2)}, u32[]{:S(2)}) collective-permute-start(bf16[12,2,4,256,128]{4,3,2,1,0:T(8,128)(2,1)} %param.13), channel_id=1, source_target_pairs={{0,1},{1,0},{2,3},{3,2},{4,5},{5,4},{6,7},{7,6},{8,9},{9,8},{10,11... | collective-permute-start | bytes 18874376 | tf_op jit(solution)/shard_map/ppermute | solution.py:21
  11.6 10.8 %collective-permute-start = (bf16[1,3,2,4,512,128]{5,4,3,1,2,0:T(8,128)(2,1)}, bf16[1,3,2,4,512,128]{5,4,3,1,2,0:T(8,128)(2,1)}, u32[]{:S(2)}, u32[]{:S(2)}) collective-permute-start(bf16[1,3,2,4,512,128]{5,4,3,1,2,0:T(8,128)(2,1)} %copy.48), channel_id=1, source_target_pairs={{0,1},{1,0},{2,3},{3,2},{4,5},{5,4},{6,7},{7,6},{8,9},{9,8},{10,11... | collective-permute-start | bytes 9437192 | tf_op jit(solution)/shard_map/ppermute | solution.py:21
  11.8 5.7 %collective-permute-start.1 = (s32[12]{0:T(128)S(1)}, s32[12]{0:T(128)S(1)}, u32[]{:S(2)}, u32[]{:S(2)}) collective-permute-start(s32[12]{0:T(128)S(1)} %copy-done.6), channel_id=1, source_target_pairs={{0,1},{1,0},{2,3},{3,2},{4,5},{5,4},{6,7},{7,6},{8,9},{9,8},{10,11... | collective-permute-start | bytes 152 | tf_op jit(solution)/shard_map/ppermute | solution.py:21
  18.7 8.7 %slice-start.2 = ((s8[6291456]{0:T(1024)(128)(4,1)}), s8[4194304]{0:T(1024)(128)(4,1)S(1)}, s32[]{:S(2)}) async-start(s8[6291456]{0:T(1024)(128)(4,1)} %bitcast.115), calls=%async_computation.7 | async-start | bytes 8388608
  19.5 8.0 %slice-start.3 = ((s8[6291456]{0:T(1024)(128)(4,1)}), s8[2097152]{0:T(1024)(128)(4,1)S(1)}, s32[]{:S(2)}) async-start(s8[6291456]{0:T(1024)(128)(4,1)} %bitcast.115), calls=%async_computation.8 | async-start | bytes 4194304
  86.0 13.5 %all-to-all-start = ((bf16[16,12,512]{2,1,0:T(8,128)(2,1)}), bf16[16,12,512]{2,1,0:T(8,128)(2,1)S(1)}, u32[]{:S(2)}, u32[]{:S(2)}) async-start(bf16[16,12,512]{2,1,0:T(8,128)(2,1)} %all_to_all.24), calls=%async_computation | async-start | bytes 524288 | tf_op jit(solution)/shard_map/all_to_all | solution.py:99
  89.5 130.6 %reduce-scatter.2.cloned.1.call-start = ((), (), s32[]{:S(2)}) async-start(), calls=%async_computation.4 | async-start | bytes 6684672 | tf_op jit(solution)/shard_map/reduce_scatter | solution.py:132
  95.7 11.3 %copy-start.1 = (bf16[3,2,4,512,128]{4,3,2,0,1:T(8,128)(2,1)S(1)}, bf16[3,2,4,512,128]{4,3,2,0,1:T(8,128)(2,1)}, u32[]{:S(2)}) copy-start(bf16[3,2,4,512,128]{4,3,2,0,1:T(8,128)(2,1)} %get-tuple-element.15) | copy-start | bytes 9437188
  101.6 5.4 %copy-start.2 = (bf16[3,2,4,512,128]{4,3,2,0,1:T(8,128)(2,1)S(1)}, bf16[3,2,4,512,128]{4,3,2,0,1:T(8,128)(2,1)}, u32[]{:S(2)}) copy-start(bf16[3,2,4,512,128]{4,3,2,0,1:T(8,128)(2,1)} %get-tuple-element.16) | copy-start | bytes 9437188
  106.6 2.5 %slice-start = ((s8[6291456]{0:T(1024)(128)(4,1)}), s8[4194304]{0:T(1024)(128)(4,1)S(1)}, s32[]{:S(2)}) async-start(s8[6291456]{0:T(1024)(128)(4,1)} %bitcast.113), calls=%async_computation.5 | async-start | bytes 8388608
  107.0 2.6 %slice-start.1 = ((s8[6291456]{0:T(1024)(128)(4,1)}), s8[2097152]{0:T(1024)(128)(4,1)S(1)}, s32[]{:S(2)}) async-start(s8[6291456]{0:T(1024)(128)(4,1)} %bitcast.113), calls=%async_computation.6 | async-start | bytes 4194304
  108.4 1.8 copy-start.4
Sparse Core Ops, SparseCore 0:
  9.6 64.6 all-gather.1
  136.6 83.5 reduce-scatter.1
where the time goes:
time: 228 us; the launch traced here: 227 us
  waiting for transfers between devices  118 us (52%)
  matrix products  29.8 us (13%)
  local copies, waits for them, and re-layouts  24.4 us (11%)
  other arithmetic  24.1 us (11%)
  between operations  13.6 us (6%)
  blocking collectives  12.8 us (6%)
  starting transfers between devices  4.64 us (2%)
    reduce_scatter x1, waiting for transfers between devices, body(): lax.psum_scatter(projected.astype(jnp.bfloat16), 'tensor', scatter_dimens...  83.7 us
    all_gather x1, waiting for transfers between devices, body(): lax.all_gather(hidden, 'tensor', axis=1, tiled=True)  22.6 us
    gather x2, local copies, waits for them, and re-layouts, body(): jnp.take_along_axis(pages_all, own_par[:, :, None, None, None, None], axi...  15 us
    all_to_all x1, blocking collectives, body(): lax.all_to_all(heads_out, 'tensor', split_axis=1, concat_axis=0, tiled=True)  12.8 us
    dot_general x1, matrix products, body(): projected = jnp.dot(heads_view, w_out, preferred_element_type=jnp.float32)  11.9 us
    dot_general x1, matrix products, body(): jnp.dot(lax.all_gather(hidden, 'tensor', axis=1, tiled=True), w_query, pr...  11 us
    select_n x3, other arithmetic, in_order(): lower_part = jnp.where(pair_side == 0, own_part_rows, far_rows)  8.91 us
    ppermute x3, waiting for transfers between devices, swapped(): return lax.ppermute(block, axis, route)  6.88 us
  transfers between devices with their start and end apart: 6, of which 5 were waited for; matrix products, arithmetic and copies ran while one was open for 19% of the time, Pallas kernels for 0%

commit v1 on v0

--- a/solution.py
+++ b/solution.py
@@ -96,7 +96,12 @@
         w_query,
         preferred_element_type=jnp.float32,
     ).astype(jnp.bfloat16)
-    local_q = lax.all_to_all(query, "tensor", split_axis=0, concat_axis=1, tiled=True)
+    local_q = jnp.concatenate(
+        lax.all_to_all(
+            jnp.stack(jnp.split(query, lax.axis_size("tensor"), axis=0)), "tensor", 0, 0
+        ),
+        axis=1,
+    )
     local_q = local_q.reshape(prompts_here, half_beams, HEADS, HD)
     own_par = parents.reshape(prompts_here, half_beams)
     own_len = lengths.reshape(prompts_here, half_beams)

time: 228 us -> 237 us (1.039)
  local copies, waits for them, and re-layouts: 24.4 us -> 33.3 us
    unnamed x23 -> x38, local copies, waits for them, and re-layouts: 4.41 us -> 13.5 us
  transfers between devices with their start and end apart: 6 -> 6, of which waited for: 5 -> 5; matrix products, arithmetic and copies ran while one was open for 19% -> 18% of each run, Pallas kernels for 0% -> 0%
where the time goes in v1:
time: 237 us; the launch traced here: 236 us
  waiting for transfers between devices  118 us (50%)
  local copies, waits for them, and re-layouts  33.3 us (14%)
  matrix products  29.8 us (13%)
  other arithmetic  24.1 us (10%)
  between operations  13.6 us (6%)
  blocking collectives  12.8 us (5%)
  starting transfers between devices  4.64 us (2%)
    reduce_scatter x1, waiting for transfers between devices, body(): lax.psum_scatter(projected.astype(jnp.bfloat16), 'tensor', scatter_dimens...  83.7 us
    all_gather x1, waiting for transfers between devices, body(): lax.all_gather(hidden, 'tensor', axis=1, tiled=True)  22.6 us
    gather x2, local copies, waits for them, and re-layouts, body(): jnp.take_along_axis(pages_all, own_par[:, :, None, None, None, None], axi...  15 us
    unnamed x38, local copies, waits for them, and re-layouts  13.5 us
    all_to_all x1, blocking collectives, body(): lax.all_to_all(heads_out, 'tensor', split_axis=1, concat_axis=0, tiled=True)  12.8 us
    dot_general x1, matrix products, body(): projected = jnp.dot(heads_view, w_out, preferred_element_type=jnp.float32)  11.9 us
    dot_general x1, matrix products, body(): jnp.dot(lax.all_gather(hidden, 'tensor', axis=1, tiled=True), w_query, pr...  11 us
    select_n x3, other arithmetic, in_order(): lower_part = jnp.where(pair_side == 0, own_part_rows, far_rows)  8.91 us
  transfers between devices with their start and end apart: 6, of which 5 were waited for; matrix products, arithmetic and copies ran while one was open for 18% of the time, Pallas kernels for 0%

profile of v1, /device:TPU:0, one launch (start us, length us, event | category | flops | bytes accessed | tf_op | source)
XLA Modules:
  0.0 236.0 jit_solution(11216684473308494828)
XLA Ops:
  6.5 0.0 all-gather.2.cloned.1.call-start
  6.6 0.7 all-gather.2.cloned.1.call-update
  7.3 0.5 collective-permute-start.2
  7.8 3.9 %copy.48 = bf16[1,3,2,4,512,128]{5,4,3,1,2,0:T(8,128)(2,1)} copy(bf16[1,3,2,4,512,128]{5,4,3,2,1,0:T(8,128)(2,1)} %param.12) | data formatting | bytes 6291456 | tf_op args[4]
  11.6 0.2 collective-permute-start
  11.8 0.3 collective-permute-start.1
  12.2 0.1 reshape.188
  12.2 0.1 reshape.187
  12.3 0.1 reshape.192
  12.4 0.6 fusion.75
  13.1 0.6 fusion.67
  13.7 3.9 %collective-permute-done.1 = s32[12]{0:T(128)S(1)} collective-permute-done((s32[12]{0:T(128)S(1)}, s32[12]{0:T(128)S(1)}, u32[]{:S(2)}, u32[]{:S(2)}) %collective-permute-start.1) | collective-permute-done | bytes 80 | tf_op jit(solution)/shard_map/ppermute | solution.py:21
  17.6 0.1 select_n.128
  17.7 0.1 select_n.126
  17.7 0.1 pad_add_fusion
  17.8 0.7 gather_fusion
  18.6 0.1 reshape.195
  18.7 0.1 iota_compare_fusion
  18.7 0.7 multiply_cosine_fusion
  19.5 3.0 %collective-permute-done = bf16[1,3,2,4,512,128]{5,4,3,1,2,0:T(8,128)(2,1)} collective-permute-done((bf16[1,3,2,4,512,128]{5,4,3,1,2,0:T(8,128)(2,1)}, bf16[1,3,2,4,512,128]{5,4,3,1,2,0:T(8,128)(2,1)}, u32[]{:S(2)}, u32[]{:S(2)}) %collective-permute-start) | collective-permute-done | bytes 3145760 | tf_op jit(solution)/shard_map/ppermute | solution.py:21
  22.4 5.0 %select_bitcast_fusion.1 = (bf16[3,2,4,512,128]{4,3,2,0,1:T(8,128)(2,1)}, bf16[3,2,4,512,128]{4,3,2,0,1:T(8,128)(2,1)}) fusion(bf16[1,3,2,4,512,128]{5,4,3,1,2,0:T(8,128)(2,1)} %collective-permute-done, pred[]{:T(512)S(6)} %eq.4, bf16[1,3,2,4,512,128]{5,4,3,2,1,0:T(8,128)(2,1)S(1)} %copy-done), kind=kLoop, calls=%fused_computation.24 | loop fusion | flops 3145728 | bytes 12582913 | tf_op jit(solution)/shard_map/jit(_where)/select_n | solution.py:90
  27.5 3.9 %broadcast_select_fusion.1 = (bf16[12,2,4,256,128]{4,3,2,1,0:T(8,128)(2,1)S(1)}, bf16[12,2,4,256,128]{4,3,2,1,0:T(8,128)(2,1)S(1)}) fusion(bf16[12,2,4,256,128]{4,3,2,1,0:T(8,128)(2,1)S(1)} %bitcast.180, bf16[12,2,4,256,128]{4,3,2,1,0:T(8,128)(2,1)} %collective-permute-done.2, pred[]{:T(512)S(6)} %eq.4), kind=kLoop, calls=%fused_computation.7 | loop fusion | flops 6291456 | bytes 25165824 | tf_op jit(solution)/shard_map/jit(_where)/select_n | solution.py:90
  31.4 5.3 %pad_maximum_fusion = bf16[3,8,2,4,256,128]{5,4,3,2,1,0:T(8,128)(2,1)} fusion(bf16[3,4,2,4,256,128]{5,4,3,2,1,0:T(8,128)(2,1)S(1)} %bitcast.176, bf16[3,4,2,4,256,128]{5,4,3,2,1,0:T(8,128)(2,1)S(1)} %bitcast.175), kind=kLoop, calls=%fused_computation.3 | loop fusion | flops 6291456 | bytes 25165824 | tf_op jit(solution)/shard_map/concatenate | solution.py:92
  36.6 8.8 %gather_fusion.1 = bf16[12,2,4,256,128]{4,3,2,1,0:T(8,128)(2,1)} fusion(bf16[3,8,2,4,256,128]{5,4,3,2,1,0:T(8,128)(2,1)} %pad_maximum_fusion, s32[12]{0:T(128)S(1)} %reshape.192), kind=kCustom, calls=%fused_computation.1 | custom fusion | bytes 12583008 | tf_op jit(solution)/shard_map/jit(take_along_axis)/gather | solution.py:115
  45.4 6.2 %copy.53 = bf16[12,2,4,256,128]{4,3,2,0,1:T(8,128)(2,1)} copy(bf16[12,2,4,256,128]{4,3,2,1,0:T(8,128)(2,1)} %gather_fusion.1) | data formatting | bytes 12582912 | tf_op jit(solution)/shard_map/jit(take_along_axis)/gather | solution.py:115
  51.7 22.6 %all-gather.2.cloned.1.call-done = bf16[192,16384]{1,0:T(8,128)(2,1)} async-done(((bf16[192,1024]{1,0:T(8,128)(2,1)}), bf16[192,16384]{1,0:T(8,128)(2,1)}) %all-gather.2.cloned.1.call-update) | async-done | bytes 6291472 | tf_op jit(solution)/shard_map/all_gather | solution.py:95
  74.2 11.0 %convolution_convert_fusion.1 = bf16[192,512]{1,0:T(8,128)(2,1)S(1)} fusion(bf16[192,16384]{1,0:T(8,128)(2,1)} %all-gather.2.cloned.1.call-done, bf16[16384,512]{1,0:T(8,128)(2,1)} %param.9), kind=kOutput, calls=%fused_computation.35 | convolution fusion | flops 3221323776 | bytes 23265280 | tf_op jit(solution)/shard_map/dot_general | solution.py:94
  85.2 0.6 constant_dynamic-update-slice_fusion.15
  85.8 0.6 constant_dynamic-update-slice_fusion.14
  86.5 0.6 constant_dynamic-update-slice_fusion.13
  87.1 0.6 constant_dynamic-update-slice_fusion.12
  87.7 0.6 constant_dynamic-update-slice_fusion.11
  88.3 0.6 constant_dynamic-update-slice_fusion.10
  88.9 0.6 constant_dynamic-update-slice_fusion.9
  89.5 0.6 constant_dynamic-update-slice_fusion.8
  90.1 0.6 constant_dynamic-update-slice_fusion.7
  90.7 0.6 constant_dynamic-update-slice_fusion.6
  91.3 0.6 constant_dynamic-update-slice_fusion.5
  91.9 0.6 constant_dynamic-update-slice_fusion.4
  92.5 0.6 constant_dynamic-update-slice_fusion.3
  93.2 0.6 constant_dynamic-update-slice_fusion.2
  93.8 0.6 constant_dynamic-update-slice_fusion.1
  94.4 0.6 constant_dynamic-update-slice_fusion
  95.0 3.5 %all-to-all-start = ((bf16[16,12,512]{2,1,0:T(8,128)(2,1)}), bf16[16,12,512]{2,1,0:T(8,128)(2,1)S(1)}, u32[]{:S(2)}, u32[]{:S(2)}) async-start(bf16[16,12,512]{2,1,0:T(8,128)(2,1)} %constant_dynamic-update-slice_fusion), calls=%async_computation | async-start | bytes 524288 | tf_op jit(solution)/shard_map/all_to_all | solution.py:100
  98.5 0.0 reduce-scatter.2.cloned.1.call-start
  98.6 6.1 %broadcast_select_fusion.2 = bf16[3,4,2,4,256,128]{5,4,3,1,0,2:T(8,128)(2,1)} fusion(bf16[3,4,2,4,256,128]{5,4,3,1,0,2:T(8,128)(2,1)} %bitcast.174, pred[3,4]{1,0:T(4,128)(4,1)S(1)} %get-tuple-element.12), kind=kLoop, calls=%fused_computation.8 | loop fusion | flops 3145728 | bytes 12582924 | tf_op jit(solution)/shard_map/jit(take_along_axis)/select_n | solution.py:115
  104.7 3.8 %all-to-all-done = bf16[16,12,512]{2,1,0:T(8,128)(2,1)S(1)} async-done(((bf16[16,12,512]{2,1,0:T(8,128)(2,1)}), bf16[16,12,512]{2,1,0:T(8,128)(2,1)S(1)}, u32[]{:S(2)}, u32[]{:S(2)}) %all-to-all-start) | async-done | bytes 196640 | tf_op jit(solution)/shard_map/all_to_all | solution.py:100
  108.6 1.0 copy.50
  109.6 1.0 reshape.190
  110.6 1.0 multiply_subtract_fusion
  111.6 0.2 fusion.56
  111.8 0.9 fusion.58
  112.7 2.9 %select_reduce_fusion = (f32[3,4,4,16]{3,2,1,0:T(4,128)S(1)}, f32[3,4,4,16,256]{4,3,2,1,0:T(8,128)S(1)}) fusion(pred[3,4,256]{2,1,0:T(4,128)(4,1)S(1)} %iota_compare_fusion, bf16[3,4,2,4,256,128]{5,4,3,1,0,2:T(8,128)(2,1)} %broadcast_select_fusion.2, bf16[3,4,4,16,128]{4,3,1,2,0:T(8,128)(2,1)S(1)} %fusion.56), kind=kOutput, calls=%fused_computation.39 | convolution fusion | flops 50724096 | bytes 4134912 | tf_op jit(solution)/shard_map/pbkge,pbkse->pbkgs/dot_general | solution.py:55
  115.7 0.4 fusion.54
  116.1 1.3 bitcast_reduce_fusion
  117.4 0.7 fusion.12
  118.1 0.5 slice-done.1
  118.6 0.5 fusion.21
  119.2 1.2 fusion.49
  120.4 0.1 all_to_all.18
  120.6 0.1 copy.61
  120.7 12.8 %all_to_all.24 = bf16[12,16,512]{2,0,1:T(8,128)(2,1)S(1)} all-to-all(bf16[12,16,512]{2,0,1:T(8,128)(2,1)S(1)} %copy.61), channel_id=1, replica_groups=mesh['groups'=2,'tensor'=16] {'tensor'}, dimensions={1} | all-to-all | bytes 393216 | tf_op jit(solution)/shard_map/all_to_all | solution.py:135
  133.6 11.9 %convolution_convert_fusion = bf16[192,16384]{1,0:T(8,128)(2,1)} fusion(bf16[192,512]{1,0:T(8,128)(2,1)S(1)} %all_to_all.21, bf16[512,16384]{1,0:T(8,128)(2,1)} %param.10), kind=kOutput, calls=%fused_computation.2 | convolution fusion | flops 3224371200 | bytes 23265280 | tf_op jit(solution)/shard_map/dot_general | solution.py:136
  145.5 83.7 %reduce-scatter.2.cloned.1.call-done = bf16[192,1024]{1,0:T(8,128)(2,1)} async-done(((bf16[192,16384]{1,0:T(8,128)(2,1)}), bf16[192,1024]{1,0:T(8,128)(2,1)}) %reduce-scatter.2.cloned.1.call-update) | async-done | bytes 393232 | tf_op jit(solution)/shard_map/reduce_scatter | solution.py:137
  (33 shorter events, 0.3 us)
Async XLA Ops:
  6.5 15.9 %copy-start = (bf16[1,3,2,4,512,128]{5,4,3,2,1,0:T(8,128)(2,1)S(1)}, bf16[1,3,2,4,512,128]{5,4,3,2,1,0:T(8,128)(2,1)}, u32[]{:S(2)}) copy-start(bf16[1,3,2,4,512,128]{5,4,3,2,1,0:T(8,128)(2,1)} %param.12) | copy-start | bytes 9437188
  6.5 5.3 %copy-start.6 = (s32[12]{0:T(128)S(1)}, s32[12]{0:T(128)}, u32[]{:S(2)}) copy-start(s32[12]{0:T(128)} %param.15) | copy-start | bytes 148
  6.5 5.6 %copy-start.5 = (s32[12]{0:T(128)S(1)}, s32[12]{0:T(128)}, u32[]{:S(2)}) copy-start(s32[12]{0:T(128)} %param.14) | copy-start | bytes 148
  6.5 5.9 %copy-start.3 = (bf16[12,2,4,128]{3,2,1,0:T(4,128)(2,1)S(1)}, bf16[12,2,4,128]{3,2,1,0:T(4,128)(2,1)}, u32[]{:S(2)}) copy-start(bf16[12,2,4,128]{3,2,1,0:T(4,128)(2,1)} %param.11) | copy-start | bytes 73732
  6.5 67.7 %all-gather.2.cloned.1.call-start = ((), (), s32[]{:S(2)}) async-start(), calls=%async_computation.3 | async-start | bytes 6684672 | tf_op jit(solution)/shard_map/all_gather | solution.py:95
  7.3 20.2 %collective-permute-start.2 = (bf16[12,2,4,256,128]{4,3,2,1,0:T(8,128)(2,1)}, bf16[12,2,4,256,128]{4,3,2,1,0:T(8,128)(2,1)}, u32[]{:S(2)}, u32[]{:S(2)}) collective-permute-start(bf16[12,2,4,256,128]{4,3,2,1,0:T(8,128)(2,1)} %param.13), channel_id=1, source_target_pairs={{0,1},{1,0},{2,3},{3,2},{4,5},{5,4},{6,7},{7,6},{8,9},{9,8},{10,11... | collective-permute-start | bytes 18874376 | tf_op jit(solution)/shard_map/ppermute | solution.py:21
  11.6 10.8 %collective-permute-start = (bf16[1,3,2,4,512,128]{5,4,3,1,2,0:T(8,128)(2,1)}, bf16[1,3,2,4,512,128]{5,4,3,1,2,0:T(8,128)(2,1)}, u32[]{:S(2)}, u32[]{:S(2)}) collective-permute-start(bf16[1,3,2,4,512,128]{5,4,3,1,2,0:T(8,128)(2,1)} %copy.48), channel_id=1, source_target_pairs={{0,1},{1,0},{2,3},{3,2},{4,5},{5,4},{6,7},{7,6},{8,9},{9,8},{10,11... | collective-permute-start | bytes 9437192 | tf_op jit(solution)/shard_map/ppermute | solution.py:21
  11.8 5.7 %collective-permute-start.1 = (s32[12]{0:T(128)S(1)}, s32[12]{0:T(128)S(1)}, u32[]{:S(2)}, u32[]{:S(2)}) collective-permute-start(s32[12]{0:T(128)S(1)} %copy-done.6), channel_id=1, source_target_pairs={{0,1},{1,0},{2,3},{3,2},{4,5},{5,4},{6,7},{7,6},{8,9},{9,8},{10,11... | collective-permute-start | bytes 152 | tf_op jit(solution)/shard_map/ppermute | solution.py:21
  18.7 8.7 %slice-start.2 = ((s8[6291456]{0:T(1024)(128)(4,1)}), s8[4194304]{0:T(1024)(128)(4,1)S(1)}, s32[]{:S(2)}) async-start(s8[6291456]{0:T(1024)(128)(4,1)} %bitcast.179), calls=%async_computation.7 | async-start | bytes 8388608
  19.5 8.0 %slice-start.3 = ((s8[6291456]{0:T(1024)(128)(4,1)}), s8[2097152]{0:T(1024)(128)(4,1)S(1)}, s32[]{:S(2)}) async-start(s8[6291456]{0:T(1024)(128)(4,1)} %bitcast.179), calls=%async_computation.8 | async-start | bytes 4194304
  95.0 13.5 %all-to-all-start = ((bf16[16,12,512]{2,1,0:T(8,128)(2,1)}), bf16[16,12,512]{2,1,0:T(8,128)(2,1)S(1)}, u32[]{:S(2)}, u32[]{:S(2)}) async-start(bf16[16,12,512]{2,1,0:T(8,128)(2,1)} %constant_dynamic-update-slice_fusion), calls=%async_computation | async-start | bytes 524288 | tf_op jit(solution)/shard_map/all_to_all | solution.py:100
  98.5 130.6 %reduce-scatter.2.cloned.1.call-start = ((), (), s32[]{:S(2)}) async-start(), calls=%async_computation.4 | async-start | bytes 6684672 | tf_op jit(solution)/shard_map/reduce_scatter | solution.py:137
  104.7 11.3 %copy-start.1 = (bf16[3,2,4,512,128]{4,3,2,0,1:T(8,128)(2,1)S(1)}, bf16[3,2,4,512,128]{4,3,2,0,1:T(8,128)(2,1)}, u32[]{:S(2)}) copy-start(bf16[3,2,4,512,128]{4,3,2,0,1:T(8,128)(2,1)} %get-tuple-element.15) | copy-start | bytes 9437188
  110.6 5.4 %copy-start.2 = (bf16[3,2,4,512,128]{4,3,2,0,1:T(8,128)(2,1)S(1)}, bf16[3,2,4,512,128]{4,3,2,0,1:T(8,128)(2,1)}, u32[]{:S(2)}) copy-start(bf16[3,2,4,512,128]{4,3,2,0,1:T(8,128)(2,1)} %get-tuple-element.16) | copy-start | bytes 9437188
  115.6 2.5 %slice-start = ((s8[6291456]{0:T(1024)(128)(4,1)}), s8[4194304]{0:T(1024)(128)(4,1)S(1)}, s32[]{:S(2)}) async-start(s8[6291456]{0:T(1024)(128)(4,1)} %bitcast.177), calls=%async_computation.5 | async-start | bytes 8388608
  116.0 2.6 %slice-start.1 = ((s8[6291456]{0:T(1024)(128)(4,1)}), s8[2097152]{0:T(1024)(128)(4,1)S(1)}, s32[]{:S(2)}) async-start(s8[6291456]{0:T(1024)(128)(4,1)} %bitcast.177), calls=%async_computation.6 | async-start | bytes 4194304
  117.4 1.8 copy-start.4
Sparse Core Ops, SparseCore 0:
  9.6 64.6 all-gather.1
  145.6 83.5 reduce-scatter.1
